TPU v7x, 512 devices: a whole 4x4x16 slice. The times are simulated.
512 devices in a mesh: gx: 32 (over x, z_hi, y), gy: 16 (over z_lo, core).
Axes of the slice: x: 4, y: 4, z: 16 (z_hi: 2, z_lo: 8; z = z_hi * 8 + z_lo), core: 2. Of those that a mesh axis runs over, the one named last changes fastest.
Arguments:
- start_vectors: bfloat16 [128, 32, 128, 128], P('gx', 'gy'), may hold values from -6 to 6
- blocks: bfloat16 [128, 32, 7, 128, 128], P('gx', 'gy'), as said below
- neighbour: int32 [128, 32, 7], P('gx', 'gy'), may hold values from 0 to 8, as said below
- counts: int32 [128, 32], P('gx', 'gy'), may hold values from 1 to 7, as said below
Outputs:
- moments: float32 [5, 128], replicated
- last_vector: bfloat16 [128, 32, 128, 128], P('gx', 'gy')
Inputs may be any that keep to these rules, and one draw needn't show every extreme that they name: `neighbour`: each tile's 7 slots name the codes 0, 1, 3, 4, 5, 7, 8 once each, its live slots first; code 4 (the tile itself) is always live; tile t couples to tile t + d through a live slot exactly when tile t + d couples to t through a live slot of the opposite code. `counts`: one plus the number of the tile's live couplings to other tiles. The block of a live coupling of tile t + d back to tile t is the transpose of the block of tile t towards t + d; blocks of code 4 are symmetric.
All inputs are finite; a program needn't handle non-finite values.
Results may differ from a plain program's by a relative error of at most 0.0045.
Values may be sent and summed in bfloat16 or wider, within the bound.
A program may use at most 64 MiB of HBM per device.

v0:
```python
import jax
import jax.numpy as jnp
from jax import lax
from jax.sharding import PartitionSpec as P

ITERS = 4


def with_halo(cells, sides, width):
    for axis, dim in sides:
        count = lax.axis_size(axis)
        head = lax.slice_in_dim(cells, 0, width, axis=dim)
        tail = lax.slice_in_dim(cells, cells.shape[dim] - width, cells.shape[dim], axis=dim)
        cells = jnp.concatenate(
            [
                lax.ppermute(tail, axis, [(i, (i + 1) % count) for i in range(count)]),
                cells,
                lax.ppermute(head, axis, [((i + 1) % count, i) for i in range(count)]),
            ],
            axis=dim,
        )
    return cells


def local_apply(extended, blocks, neighbour, counts):
    tiles_x, tiles_y, slots = neighbour.shape
    vectors, orbitals = (extended.shape[2], extended.shape[3])
    flat = extended.reshape((tiles_x + 2) * (tiles_y + 2), vectors, orbitals)
    xs = jnp.arange(tiles_x, dtype=jnp.int32)[:, None] + 1
    ys = jnp.arange(tiles_y, dtype=jnp.int32)[None, :] + 1
    total = jnp.zeros((tiles_x, tiles_y, vectors, orbitals), jnp.float32)
    for slot in range(slots):
        code = neighbour[:, :, slot]
        index = (xs + code // 3 - 1) * (tiles_y + 2) + (ys + code % 3 - 1)
        piece = jnp.take(flat, index, axis=0)
        product = jnp.einsum(
            "xyrb,xyba->xyra", piece, blocks[:, :, slot], preferred_element_type=jnp.float32
        )
        live = (slot < counts).astype(jnp.float32)[:, :, None, None]
        total = total + live * product
    return total


def extend(vectors):
    along_x = with_halo(vectors, (("gx", 0),), 1)
    return with_halo(along_x, (("gy", 1),), 1)


def on_device(start_vectors, blocks, neighbour, counts):
    tiles_x, tiles_y = counts.shape
    total_rows = (
        tiles_x * lax.axis_size("gx") * tiles_y * lax.axis_size("gy") * start_vectors.shape[3]
    )
    first = start_vectors.astype(jnp.float32)
    partials = [jnp.sum(first * first, axis=(0, 1, 3))]
    previous = first
    current = local_apply(extend(start_vectors), blocks, neighbour, counts)
    partials.append(jnp.sum(first * current, axis=(0, 1, 3)))
    for step in range(ITERS - 1):
        image = local_apply(extend(current.astype(jnp.bfloat16)), blocks, neighbour, counts)
        following = 2.0 * image - previous
        previous, current = (current, following)
        partials.append(jnp.sum(first * current, axis=(0, 1, 3)))
    summed = jnp.stack([lax.psum(term, ("gx", "gy")) for term in partials])
    return (summed / total_rows, current.astype(jnp.bfloat16))


def solution(mesh):
    in_specs = (
        P("gx", "gy", None, None),
        P("gx", "gy", None, None, None),
        P("gx", "gy", None),
        P("gx", "gy"),
    )
    out_specs = (P(), P("gx", "gy", None, None))
    return jax.shard_map(
        on_device, mesh=mesh, in_specs=in_specs, out_specs=out_specs, check_vma=False
    )
```

profile of v0, /device:TPU:1, one launch (start us, length us, event | category | flops | bytes accessed | tf_op | source)
XLA Modules:
  0.0 365.0 jit_solution(12642964493823538940)
XLA Ops:
  1.5 4.0 %collective-permute-start = (bf16[1,2,128,128]{3,2,1,0:T(8,128)(2,1)S(1)}, bf16[1,2,128,128]{3,2,1,0:T(8,128)(2,1)S(1)}, u32[]{:S(2)}, u32[]{:S(2)}) collective-permute-start(bf16[1,2,128,128]{3,2,1,0:T(8,128)(2,1)S(1)} %get-tuple-element.49), channel_id=1, source_target_pairs={{0,16},{16,32},{32,48},{48,64},{64,80},{80,96},{96,112},{112,128},... | collective-permute-start | bytes 196616 | tf_op jit(solution)/shard_map/ppermute | solution.py:16
  5.6 18.8 %collective-permute-start.1 = (bf16[1,2,128,128]{3,2,1,0:T(8,128)(2,1)S(1)}, bf16[1,2,128,128]{3,2,1,0:T(8,128)(2,1)S(1)}, u32[]{:S(2)}, u32[]{:S(2)}) collective-permute-start(bf16[1,2,128,128]{3,2,1,0:T(8,128)(2,1)S(1)} %get-tuple-element.48), channel_id=1, source_target_pairs={{16,0},{32,16},{48,32},{64,48},{80,64},{96,80},{112,96},{128,112},... | collective-permute-start | bytes 196616 | tf_op jit(solution)/shard_map/ppermute | solution.py:18
  32.2 4.7 %collective-permute-start.3 = (bf16[6,1,128,128]{3,2,1,0:T(8,128)(2,1)S(1)}, bf16[6,1,128,128]{3,2,1,0:T(8,128)(2,1)S(1)}, u32[]{:S(2)}, u32[]{:S(2)}) collective-permute-start(bf16[6,1,128,128]{3,2,1,0:T(8,128)(2,1)S(1)} %get-tuple-element.41), channel_id=1, source_target_pairs={{1,0},{2,1},{3,2},{4,3},{5,4},{6,5},{7,6},{8,7},{9,8},{10,9},{11,1... | collective-permute-start | bytes 589832 | tf_op jit(solution)/shard_map/ppermute | solution.py:18
  36.9 1.9 collective-permute-start.2
  39.2 5.3 %collective-permute-done.2 = bf16[6,1,128,128]{3,2,1,0:T(8,128)(2,1)S(1)} collective-permute-done((bf16[6,1,128,128]{3,2,1,0:T(8,128)(2,1)S(1)}, bf16[6,1,128,128]{3,2,1,0:T(8,128)(2,1)S(1)}, u32[]{:S(2)}, u32[]{:S(2)}) %collective-permute-start.2) | collective-permute-done | bytes 196640 | tf_op jit(solution)/shard_map/ppermute | solution.py:16
  56.4 12.2 %collective-permute-start.5 = (bf16[1,2,128,128]{2,3,1,0:T(8,128)(2,1)S(1)}, bf16[1,2,128,128]{2,3,1,0:T(8,128)(2,1)S(1)}, u32[]{:S(2)}, u32[]{:S(2)}) collective-permute-start(bf16[1,2,128,128]{2,3,1,0:T(8,128)(2,1)S(1)} %get-tuple-element.47), channel_id=1, source_target_pairs={{16,0},{32,16},{48,32},{64,48},{80,64},{96,80},{112,96},{128,112},... | collective-permute-start | bytes 196616 | tf_op jit(solution)/shard_map/ppermute | solution.py:18
  68.6 1.9 collective-permute-start.4
  70.5 2.8 collective-permute-done.5
  73.3 13.4 %collective-permute-done.4 = bf16[1,2,128,128]{2,3,1,0:T(8,128)(2,1)S(1)} collective-permute-done((bf16[1,2,128,128]{2,3,1,0:T(8,128)(2,1)S(1)}, bf16[1,2,128,128]{2,3,1,0:T(8,128)(2,1)S(1)}, u32[]{:S(2)}, u32[]{:S(2)}) %collective-permute-start.4) | collective-permute-done | bytes 65568 | tf_op jit(solution)/shard_map/ppermute | solution.py:16
  87.4 12.2 %collective-permute-start.7 = (bf16[6,1,128,128]{2,3,1,0:T(8,128)(2,1)}, bf16[6,1,128,128]{2,3,1,0:T(8,128)(2,1)S(1)}, u32[]{:S(2)}, u32[]{:S(2)}) collective-permute-start(bf16[6,1,128,128]{2,3,1,0:T(8,128)(2,1)} %get-tuple-element.39), channel_id=1, source_target_pairs={{1,0},{2,1},{3,2},{4,3},{5,4},{6,5},{7,6},{8,7},{9,8},{10,9},{11,1... | collective-permute-start | bytes 589832 | tf_op jit(solution)/shard_map/ppermute | solution.py:18
  99.6 1.9 collective-permute-start.6
  103.1 1.6 collective-permute-done.6
  106.6 1.4 gather_fusion.8
  108.0 1.4 gather_fusion.9
  109.4 1.4 gather_fusion.10
  110.8 1.4 gather_fusion.11
  112.2 1.4 gather_fusion.12
  117.2 1.8 copy.264
  119.0 1.8 copy.265
  120.8 1.8 copy.266
  122.6 1.8 copy.267
  131.5 1.9 collective-permute-start.9
  133.5 3.4 collective-permute-start.8
  136.9 14.6 %collective-permute-done.8 = bf16[1,2,128,128]{2,3,1,0:T(8,128)(2,1)S(1)} collective-permute-done((bf16[1,2,128,128]{2,3,1,0:T(8,128)(2,1)S(1)}, bf16[1,2,128,128]{2,3,1,0:T(8,128)(2,1)S(1)}, u32[]{:S(2)}, u32[]{:S(2)}) %collective-permute-start.8) | collective-permute-done | bytes 65568 | tf_op jit(solution)/shard_map/ppermute | solution.py:16
  151.6 11.8 %collective-permute-start.11 = (bf16[6,1,128,128]{2,3,1,0:T(8,128)(2,1)S(1)}, bf16[6,1,128,128]{2,3,1,0:T(8,128)(2,1)S(1)}, u32[]{:S(2)}, u32[]{:S(2)}) collective-permute-start(bf16[6,1,128,128]{2,3,1,0:T(8,128)(2,1)S(1)} %get-tuple-element.37), channel_id=1, source_target_pairs={{1,0},{2,1},{3,2},{4,3},{5,4},{6,5},{7,6},{8,7},{9,8},{10,9},{11,1... | collective-permute-start | bytes 589832 | tf_op jit(solution)/shard_map/ppermute | solution.py:18
  163.3 1.9 collective-permute-start.10
  165.3 2.9 collective-permute-done.10
  177.3 1.8 copy.270
  180.5 1.8 copy.271
  182.3 1.8 copy.272
  184.1 1.8 copy.273
  185.9 1.8 copy.274
  189.7 1.4 fusion.15
  191.1 1.4 fusion.14
  195.0 1.9 collective-permute-start.13
  196.9 3.4 collective-permute-start.12
  200.3 14.7 %collective-permute-done.12 = bf16[1,2,128,128]{2,3,1,0:T(8,128)(2,1)S(1)} collective-permute-done((bf16[1,2,128,128]{2,3,1,0:T(8,128)(2,1)S(1)}, bf16[1,2,128,128]{2,3,1,0:T(8,128)(2,1)S(1)}, u32[]{:S(2)}, u32[]{:S(2)}) %collective-permute-start.12) | collective-permute-done | bytes 65568 | tf_op jit(solution)/shard_map/ppermute | solution.py:16
  215.1 11.8 %collective-permute-start.15 = (bf16[6,1,128,128]{2,3,1,0:T(8,128)(2,1)S(1)}, bf16[6,1,128,128]{2,3,1,0:T(8,128)(2,1)S(1)}, u32[]{:S(2)}, u32[]{:S(2)}) collective-permute-start(bf16[6,1,128,128]{2,3,1,0:T(8,128)(2,1)S(1)} %get-tuple-element.35), channel_id=1, source_target_pairs={{1,0},{2,1},{3,2},{4,3},{5,4},{6,5},{7,6},{8,7},{9,8},{10,9},{11,1... | collective-permute-start | bytes 589832 | tf_op jit(solution)/shard_map/ppermute | solution.py:18
  226.9 2.1 collective-permute-start.14
  229.0 2.8 collective-permute-done.14
  240.9 1.8 copy.277
  244.1 1.8 copy.278
  246.7 1.8 copy.280
  248.5 1.8 copy.281
  250.3 1.8 copy.282
  253.2 1.4 fusion.7
  254.6 1.4 fusion.6
  258.1 105.4 %all-reduce = (f32[1,128]{1,0:T(1,128)S(1)}, f32[1,128]{1,0:T(1,128)S(1)}, f32[1,128]{1,0:T(1,128)S(1)}, f32[1,128]{1,0:T(1,128)S(1)}, f32[1,128]{1,0:T(1,128)S(1)}) all-reduce(f32[1,128]{1,0:T(1,128)S(1)} %bitcast.259, f32[1,128]{1,0:T(1,128)S(1)} %bitcast.256, ...), channel_id=1, replica_groups=mesh['gx'=32,'gy'=16] {'gx','gy'}, use_global_device_ids=true, to_apply=%region_1.2 | all-reduce | flops 640 | bytes 5120 | tf_op jit(solution)/shard_map/psum | solution.py:64
  (261 shorter events, 66.3 us)
Async XLA Ops:
  1.5 29.6 %collective-permute-start = (bf16[1,2,128,128]{3,2,1,0:T(8,128)(2,1)S(1)}, bf16[1,2,128,128]{3,2,1,0:T(8,128)(2,1)S(1)}, u32[]{:S(2)}, u32[]{:S(2)}) collective-permute-start(bf16[1,2,128,128]{3,2,1,0:T(8,128)(2,1)S(1)} %get-tuple-element.49), channel_id=1, source_target_pairs={{0,16},{16,32},{32,48},{48,64},{64,80},{80,96},{96,112},{112,128},... | collective-permute-start | bytes 196616 | tf_op jit(solution)/shard_map/ppermute | solution.py:16
  5.6 26.5 %collective-permute-start.1 = (bf16[1,2,128,128]{3,2,1,0:T(8,128)(2,1)S(1)}, bf16[1,2,128,128]{3,2,1,0:T(8,128)(2,1)S(1)}, u32[]{:S(2)}, u32[]{:S(2)}) collective-permute-start(bf16[1,2,128,128]{3,2,1,0:T(8,128)(2,1)S(1)} %get-tuple-element.48), channel_id=1, source_target_pairs={{16,0},{32,16},{48,32},{64,48},{80,64},{96,80},{112,96},{128,112},... | collective-permute-start | bytes 196616 | tf_op jit(solution)/shard_map/ppermute | solution.py:18
  28.4 23.2 %copy-start.52 = (pred[4,2]{1,0:T(4,128)(4,1)}, pred[4,2]{1,0:T(4,128)(4,1)S(1)}, u32[]{:S(2)}) copy-start(pred[4,2]{1,0:T(4,128)(4,1)S(1)} %get-tuple-element.74) | copy-start | bytes 28
  28.4 27.2 %copy-start.50 = (pred[4,2]{1,0:T(4,128)(4,1)}, pred[4,2]{1,0:T(4,128)(4,1)S(1)}, u32[]{:S(2)}) copy-start(pred[4,2]{1,0:T(4,128)(4,1)S(1)} %get-tuple-element.21) | copy-start | bytes 28
  30.0 22.9 %copy-start.48 = (pred[4,2]{1,0:T(4,128)(4,1)}, pred[4,2]{1,0:T(4,128)(4,1)S(1)}, u32[]{:S(2)}) copy-start(pred[4,2]{1,0:T(4,128)(4,1)S(1)} %get-tuple-element.64) | copy-start | bytes 28
  30.0 24.3 %copy-start.46 = (pred[4,2]{1,0:T(4,128)(4,1)}, pred[4,2]{1,0:T(4,128)(4,1)S(1)}, u32[]{:S(2)}) copy-start(pred[4,2]{1,0:T(4,128)(4,1)S(1)} %get-tuple-element.66) | copy-start | bytes 28
  30.1 24.7 %copy-start.44 = (pred[4,2]{1,0:T(4,128)(4,1)}, pred[4,2]{1,0:T(4,128)(4,1)S(1)}, u32[]{:S(2)}) copy-start(pred[4,2]{1,0:T(4,128)(4,1)S(1)} %get-tuple-element.68) | copy-start | bytes 28
  30.1 25.1 %copy-start.42 = (pred[4,2]{1,0:T(4,128)(4,1)}, pred[4,2]{1,0:T(4,128)(4,1)S(1)}, u32[]{:S(2)}) copy-start(pred[4,2]{1,0:T(4,128)(4,1)S(1)} %get-tuple-element.70) | copy-start | bytes 28
  30.1 25.9 %copy-start.54 = (pred[4,2]{1,0:T(4,128)(4,1)}, pred[4,2]{1,0:T(4,128)(4,1)S(1)}, u32[]{:S(2)}) copy-start(pred[4,2]{1,0:T(4,128)(4,1)S(1)} %get-tuple-element.19) | copy-start | bytes 28
  30.9 25.0 %copy-start.26 = (f32[4,2]{1,0:T(4,128)}, f32[4,2]{1,0:T(4,128)S(1)}, u32[]{:S(2)}) copy-start(f32[4,2]{1,0:T(4,128)S(1)} %copy.253) | copy-start | bytes 100
  31.0 14.9 %copy-start.30 = (s32[1024]{0:T(1024)}, s32[1024]{0:T(1024)S(1)}, u32[]{:S(2)}) copy-start(s32[1024]{0:T(1024)S(1)} %get-tuple-element.100) | copy-start | bytes 12292
  31.0 16.2 %copy-start.28 = (s32[1024]{0:T(1024)}, s32[1024]{0:T(1024)S(1)}, u32[]{:S(2)}) copy-start(s32[1024]{0:T(1024)S(1)} %get-tuple-element.99) | copy-start | bytes 12292
  31.0 17.5 %copy-start.34 = (s32[1024]{0:T(1024)}, s32[1024]{0:T(1024)S(1)}, u32[]{:S(2)}) copy-start(s32[1024]{0:T(1024)S(1)} %get-tuple-element.98) | copy-start | bytes 12292
  31.0 18.7 %copy-start.32 = (s32[1024]{0:T(1024)}, s32[1024]{0:T(1024)S(1)}, u32[]{:S(2)}) copy-start(s32[1024]{0:T(1024)S(1)} %get-tuple-element.97) | copy-start | bytes 12292
  31.0 19.3 %copy-start.38 = (s32[1024]{0:T(1024)}, s32[1024]{0:T(1024)S(1)}, u32[]{:S(2)}) copy-start(s32[1024]{0:T(1024)S(1)} %get-tuple-element.96) | copy-start | bytes 12292
  31.0 19.9 %copy-start.36 = (s32[1024]{0:T(1024)}, s32[1024]{0:T(1024)S(1)}, u32[]{:S(2)}) copy-start(s32[1024]{0:T(1024)S(1)} %get-tuple-element.95) | copy-start | bytes 12292
  31.1 14.8 %copy-start.40 = (s32[1024]{0:T(1024)}, s32[1024]{0:T(1024)S(1)}, u32[]{:S(2)}) copy-start(s32[1024]{0:T(1024)S(1)} %pad_clamp_fusion.6) | copy-start | bytes 12292
  32.2 7.1 %collective-permute-start.3 = (bf16[6,1,128,128]{3,2,1,0:T(8,128)(2,1)S(1)}, bf16[6,1,128,128]{3,2,1,0:T(8,128)(2,1)S(1)}, u32[]{:S(2)}, u32[]{:S(2)}) collective-permute-start(bf16[6,1,128,128]{3,2,1,0:T(8,128)(2,1)S(1)} %get-tuple-element.41), channel_id=1, source_target_pairs={{1,0},{2,1},{3,2},{4,3},{5,4},{6,5},{7,6},{8,7},{9,8},{10,9},{11,1... | collective-permute-start | bytes 589832 | tf_op jit(solution)/shard_map/ppermute | solution.py:18
  36.9 7.6 %collective-permute-start.2 = (bf16[6,1,128,128]{3,2,1,0:T(8,128)(2,1)S(1)}, bf16[6,1,128,128]{3,2,1,0:T(8,128)(2,1)S(1)}, u32[]{:S(2)}, u32[]{:S(2)}) collective-permute-start(bf16[6,1,128,128]{3,2,1,0:T(8,128)(2,1)S(1)} %get-tuple-element.40), channel_id=1, source_target_pairs={{0,1},{1,2},{2,3},{3,4},{4,5},{5,6},{6,7},{7,8},{8,9},{9,10},{10,1... | collective-permute-start | bytes 589832 | tf_op jit(solution)/shard_map/ppermute | solution.py:16
  38.8 12.7 %copy-start.24 = (f32[4,2]{1,0:T(4,128)}, f32[4,2]{1,0:T(4,128)S(1)}, u32[]{:S(2)}) copy-start(f32[4,2]{1,0:T(4,128)S(1)} %get-tuple-element.59) | copy-start | bytes 100
  38.8 15.9 %copy-start.22 = (f32[4,2]{1,0:T(4,128)}, f32[4,2]{1,0:T(4,128)S(1)}, u32[]{:S(2)}) copy-start(f32[4,2]{1,0:T(4,128)S(1)} %get-tuple-element.58) | copy-start | bytes 100
  44.6 7.0 %copy-start = (bf16[4,2,7,128,128]{4,3,2,1,0:T(8,128)(2,1)S(1)}, bf16[4,2,7,128,128]{4,3,2,1,0:T(8,128)(2,1)}, u32[]{:S(2)}) copy-start(bf16[4,2,7,128,128]{4,3,2,1,0:T(8,128)(2,1)} %param.7) | copy-start | bytes 5505028
  55.9 45.6 %copy-start.4 = (bf16[4,2,128,128]{3,2,1,0:T(8,128)(2,1)S(1)}, bf16[4,2,128,128]{3,2,1,0:T(8,128)(2,1)}, u32[]{:S(2)}) copy-start(bf16[4,2,128,128]{3,2,1,0:T(8,128)(2,1)} %param.6) | copy-start | bytes 786436
  56.4 16.9 %collective-permute-start.5 = (bf16[1,2,128,128]{2,3,1,0:T(8,128)(2,1)S(1)}, bf16[1,2,128,128]{2,3,1,0:T(8,128)(2,1)S(1)}, u32[]{:S(2)}, u32[]{:S(2)}) collective-permute-start(bf16[1,2,128,128]{2,3,1,0:T(8,128)(2,1)S(1)} %get-tuple-element.47), channel_id=1, source_target_pairs={{16,0},{32,16},{48,32},{64,48},{80,64},{96,80},{112,96},{128,112},... | collective-permute-start | bytes 196616 | tf_op jit(solution)/shard_map/ppermute | solution.py:18
  68.6 18.1 %collective-permute-start.4 = (bf16[1,2,128,128]{2,3,1,0:T(8,128)(2,1)S(1)}, bf16[1,2,128,128]{2,3,1,0:T(8,128)(2,1)S(1)}, u32[]{:S(2)}, u32[]{:S(2)}) collective-permute-start(bf16[1,2,128,128]{2,3,1,0:T(8,128)(2,1)S(1)} %get-tuple-element.46), channel_id=1, source_target_pairs={{0,16},{16,32},{32,48},{48,64},{64,80},{80,96},{96,112},{112,128},... | collective-permute-start | bytes 196616 | tf_op jit(solution)/shard_map/ppermute | solution.py:16
  87.4 15.0 %collective-permute-start.7 = (bf16[6,1,128,128]{2,3,1,0:T(8,128)(2,1)}, bf16[6,1,128,128]{2,3,1,0:T(8,128)(2,1)S(1)}, u32[]{:S(2)}, u32[]{:S(2)}) collective-permute-start(bf16[6,1,128,128]{2,3,1,0:T(8,128)(2,1)} %get-tuple-element.39), channel_id=1, source_target_pairs={{1,0},{2,1},{3,2},{4,3},{5,4},{6,5},{7,6},{8,7},{9,8},{10,9},{11,1... | collective-permute-start | bytes 589832 | tf_op jit(solution)/shard_map/ppermute | solution.py:18
  99.6 5.1 %collective-permute-start.6 = (bf16[6,1,128,128]{2,3,1,0:T(8,128)(2,1)S(1)}, bf16[6,1,128,128]{2,3,1,0:T(8,128)(2,1)}, u32[]{:S(2)}, u32[]{:S(2)}) collective-permute-start(bf16[6,1,128,128]{2,3,1,0:T(8,128)(2,1)S(1)} %get-tuple-element.38), channel_id=1, source_target_pairs={{0,1},{1,2},{2,3},{3,4},{4,5},{5,6},{6,7},{7,8},{8,9},{9,10},{10,1... | collective-permute-start | bytes 589832 | tf_op jit(solution)/shard_map/ppermute | solution.py:16
  105.8 7.8 %copy-start.37 = (s32[1024]{0:T(1024)S(1)}, s32[1024]{0:T(1024)}, u32[]{:S(2)}) copy-start(s32[1024]{0:T(1024)} %copy-done.36) | copy-start | bytes 12292
  106.6 9.2 %copy-start.25 = (f32[4,2]{1,0:T(4,128)S(1)}, f32[4,2]{1,0:T(4,128)}, u32[]{:S(2)}) copy-start(f32[4,2]{1,0:T(4,128)} %copy-done.24) | copy-start | bytes 100
  106.6 9.2 %copy-start.53 = (pred[4,2]{1,0:T(4,128)(4,1)S(1)}, pred[4,2]{1,0:T(4,128)(4,1)}, u32[]{:S(2)}) copy-start(pred[4,2]{1,0:T(4,128)(4,1)} %copy-done.52) | copy-start | bytes 28
  114.9 9.5 %copy-start.7 = (bf16[8,128,128]{1,2,0:T(8,128)(2,1)S(1)}, bf16[8,128,128]{1,2,0:T(8,128)(2,1)}, u32[]{:S(2)}) copy-start(bf16[8,128,128]{1,2,0:T(8,128)(2,1)} %gather_fusion.12) | copy-start | bytes 786436
  115.8 9.5 %copy-start.6 = (bf16[8,128,128]{1,2,0:T(8,128)(2,1)S(1)}, bf16[8,128,128]{1,2,0:T(8,128)(2,1)}, u32[]{:S(2)}) copy-start(bf16[8,128,128]{1,2,0:T(8,128)(2,1)} %gather_fusion.13) | copy-start | bytes 786436
  117.2 8.9 %copy-start.49 = (pred[4,2]{1,0:T(4,128)(4,1)S(1)}, pred[4,2]{1,0:T(4,128)(4,1)}, u32[]{:S(2)}) copy-start(pred[4,2]{1,0:T(4,128)(4,1)} %copy-done.48) | copy-start | bytes 28
  131.5 36.8 %copy-start.41 = (s32[1024]{0:T(1024)S(1)}, s32[1024]{0:T(1024)}, u32[]{:S(2)}) copy-start(s32[1024]{0:T(1024)} %copy-done.40) | copy-start | bytes 12292
  131.5 5.3 %collective-permute-start.9 = (bf16[1,2,128,128]{2,3,1,0:T(8,128)(2,1)S(1)}, bf16[1,2,128,128]{2,3,1,0:T(8,128)(2,1)S(1)}, u32[]{:S(2)}, u32[]{:S(2)}) collective-permute-start(bf16[1,2,128,128]{2,3,1,0:T(8,128)(2,1)S(1)} %get-tuple-element.45), channel_id=1, source_target_pairs={{16,0},{32,16},{48,32},{64,48},{80,64},{96,80},{112,96},{128,112},... | collective-permute-start | bytes 196616 | tf_op jit(solution)/shard_map/ppermute | solution.py:18
  133.5 36.1 %copy-start.31 = (s32[1024]{0:T(1024)S(1)}, s32[1024]{0:T(1024)}, u32[]{:S(2)}) copy-start(s32[1024]{0:T(1024)} %copy-done.30) | copy-start | bytes 12292
  133.5 18.0 %collective-permute-start.8 = (bf16[1,2,128,128]{2,3,1,0:T(8,128)(2,1)S(1)}, bf16[1,2,128,128]{2,3,1,0:T(8,128)(2,1)S(1)}, u32[]{:S(2)}, u32[]{:S(2)}) collective-permute-start(bf16[1,2,128,128]{2,3,1,0:T(8,128)(2,1)S(1)} %get-tuple-element.44), channel_id=1, source_target_pairs={{0,16},{16,32},{32,48},{48,64},{64,80},{80,96},{96,112},{112,128},... | collective-permute-start | bytes 196616 | tf_op jit(solution)/shard_map/ppermute | solution.py:16
  151.5 19.4 %copy-start.29 = (s32[1024]{0:T(1024)S(1)}, s32[1024]{0:T(1024)}, u32[]{:S(2)}) copy-start(s32[1024]{0:T(1024)} %copy-done.28) | copy-start | bytes 12292
  151.5 20.7 %copy-start.35 = (s32[1024]{0:T(1024)S(1)}, s32[1024]{0:T(1024)}, u32[]{:S(2)}) copy-start(s32[1024]{0:T(1024)} %copy-done.34) | copy-start | bytes 12292
  151.6 13.7 %collective-permute-start.11 = (bf16[6,1,128,128]{2,3,1,0:T(8,128)(2,1)S(1)}, bf16[6,1,128,128]{2,3,1,0:T(8,128)(2,1)S(1)}, u32[]{:S(2)}, u32[]{:S(2)}) collective-permute-start(bf16[6,1,128,128]{2,3,1,0:T(8,128)(2,1)S(1)} %get-tuple-element.37), channel_id=1, source_target_pairs={{1,0},{2,1},{3,2},{4,3},{5,4},{6,5},{7,6},{8,7},{9,8},{10,9},{11,1... | collective-permute-start | bytes 589832 | tf_op jit(solution)/shard_map/ppermute | solution.py:18
  163.3 10.2 %copy-start.33 = (s32[1024]{0:T(1024)S(1)}, s32[1024]{0:T(1024)}, u32[]{:S(2)}) copy-start(s32[1024]{0:T(1024)} %copy-done.32) | copy-start | bytes 12292
  163.3 11.4 %copy-start.39 = (s32[1024]{0:T(1024)S(1)}, s32[1024]{0:T(1024)}, u32[]{:S(2)}) copy-start(s32[1024]{0:T(1024)} %copy-done.38) | copy-start | bytes 12292
  163.3 4.9 %collective-permute-start.10 = (bf16[6,1,128,128]{2,3,1,0:T(8,128)(2,1)S(1)}, bf16[6,1,128,128]{2,3,1,0:T(8,128)(2,1)S(1)}, u32[]{:S(2)}, u32[]{:S(2)}) collective-permute-start(bf16[6,1,128,128]{2,3,1,0:T(8,128)(2,1)S(1)} %get-tuple-element.36), channel_id=1, source_target_pairs={{0,1},{1,2},{2,3},{3,4},{4,5},{5,6},{6,7},{7,8},{8,9},{9,10},{10,1... | collective-permute-start | bytes 589832 | tf_op jit(solution)/shard_map/ppermute | solution.py:16
  177.3 10.4 %copy-start.8 = (bf16[8,128,128]{1,2,0:T(8,128)(2,1)S(1)}, bf16[8,128,128]{1,2,0:T(8,128)(2,1)}, u32[]{:S(2)}) copy-start(bf16[8,128,128]{1,2,0:T(8,128)(2,1)} %gather_fusion.19) | copy-start | bytes 786436
  195.0 5.3 %collective-permute-start.13 = (bf16[1,2,128,128]{2,3,1,0:T(8,128)(2,1)S(1)}, bf16[1,2,128,128]{2,3,1,0:T(8,128)(2,1)S(1)}, u32[]{:S(2)}, u32[]{:S(2)}) collective-permute-start(bf16[1,2,128,128]{2,3,1,0:T(8,128)(2,1)S(1)} %get-tuple-element.43), channel_id=1, source_target_pairs={{16,0},{32,16},{48,32},{64,48},{80,64},{96,80},{112,96},{128,112},... | collective-permute-start | bytes 196616 | tf_op jit(solution)/shard_map/ppermute | solution.py:18
  196.9 18.1 %collective-permute-start.12 = (bf16[1,2,128,128]{2,3,1,0:T(8,128)(2,1)S(1)}, bf16[1,2,128,128]{2,3,1,0:T(8,128)(2,1)S(1)}, u32[]{:S(2)}, u32[]{:S(2)}) collective-permute-start(bf16[1,2,128,128]{2,3,1,0:T(8,128)(2,1)S(1)} %get-tuple-element.42), channel_id=1, source_target_pairs={{0,16},{16,32},{32,48},{48,64},{64,80},{80,96},{96,112},{112,128},... | collective-permute-start | bytes 196616 | tf_op jit(solution)/shard_map/ppermute | solution.py:16
  215.1 13.9 %collective-permute-start.15 = (bf16[6,1,128,128]{2,3,1,0:T(8,128)(2,1)S(1)}, bf16[6,1,128,128]{2,3,1,0:T(8,128)(2,1)S(1)}, u32[]{:S(2)}, u32[]{:S(2)}) collective-permute-start(bf16[6,1,128,128]{2,3,1,0:T(8,128)(2,1)S(1)} %get-tuple-element.35), channel_id=1, source_target_pairs={{1,0},{2,1},{3,2},{4,3},{5,4},{6,5},{7,6},{8,7},{9,8},{10,9},{11,1... | collective-permute-start | bytes 589832 | tf_op jit(solution)/shard_map/ppermute | solution.py:18
  226.9 4.9 %collective-permute-start.14 = (bf16[6,1,128,128]{2,3,1,0:T(8,128)(2,1)S(1)}, bf16[6,1,128,128]{2,3,1,0:T(8,128)(2,1)S(1)}, u32[]{:S(2)}, u32[]{:S(2)}) collective-permute-start(bf16[6,1,128,128]{2,3,1,0:T(8,128)(2,1)S(1)} %get-tuple-element.34), channel_id=1, source_target_pairs={{0,1},{1,2},{2,3},{3,4},{4,5},{5,6},{6,7},{7,8},{8,9},{9,10},{10,1... | collective-permute-start | bytes 589832 | tf_op jit(solution)/shard_map/ppermute | solution.py:16
  (24 other events, 50.8 us)
where the time goes:
time: 367 us; the launch traced here: 365 us
  blocking collectives  105 us (29%)
  starting transfers between devices  95.8 us (26%)
  local copies, waits for them, and re-layouts  77.4 us (21%)
  waiting for transfers between devices  58.4 us (16%)
  matrix products  23.2 us (6%)
    psum x1, blocking collectives, on_device(): summed = jnp.stack([lax.psum(term, ('gx', 'gy')) for term in partials])  105 us
    ppermute x8, starting transfers between devices, with_halo(): lax.ppermute(head, axis, [((i + 1) % count, i) for i in range(count)])  75.3 us
    gather x49, local copies, waits for them, and re-layouts, local_apply(): piece = jnp.take(flat, index, axis=0)  65.7 us
    ppermute x8, waiting for transfers between devices, with_halo(): lax.ppermute(tail, axis, [(i, (i + 1) % count) for i in range(count)])  55.2 us
    dot_general x28, matrix products, local_apply(): jnp.einsum('xyrb,xyba->xyra', piece, blocks[:, :, slot], preferred_elemen...  23.2 us
    ppermute x8, starting transfers between devices, with_halo(): lax.ppermute(tail, axis, [(i, (i + 1) % count) for i in range(count)])  20.5 us
  transfers between devices with their start and end apart: 16, of which 9 were waited for; matrix products, arithmetic and copies ran while one was open for 2% of the time, Pallas kernels for 0%

commit v1 on v0

--- a/solution.py
+++ b/solution.py
@@ -4,6 +4,11 @@
 from jax.sharding import PartitionSpec as P
 
 ITERS = 4
+
+
+def by_each_axis(value, leading, second):
+    half = lax.psum(value, leading)
+    return lax.psum(half, second)
 
 
 def with_halo(cells, sides, width):
@@ -61,7 +66,7 @@
         following = 2.0 * image - previous
         previous, current = (current, following)
         partials.append(jnp.sum(first * current, axis=(0, 1, 3)))
-    summed = jnp.stack([lax.psum(term, ("gx", "gy")) for term in partials])
+    summed = jnp.stack([by_each_axis(term, "gy", "gx") for term in partials])
     return (summed / total_rows, current.astype(jnp.bfloat16))
 
 

time: 367 us -> 461 us (1.26)
  the two profiles are of different devices: /device:TPU:1 before, /device:TPU:8 now
where the time goes in v1:
time: 461 us; the launch traced here: 459 us
  blocking collectives  205 us (44%)
  starting transfers between devices  86 us (19%)
  local copies, waits for them, and re-layouts  77.6 us (17%)
  waiting for transfers between devices  63 us (14%)
  matrix products  23.2 us (5%)
    psum x1, blocking collectives, by_each_axis(): return lax.psum(half, second)  160 us
    ppermute x8, starting transfers between devices, with_halo(): lax.ppermute(head, axis, [((i + 1) % count, i) for i in range(count)])  67.5 us
    gather x49, local copies, waits for them, and re-layouts, local_apply(): piece = jnp.take(flat, index, axis=0)  66 us
    ppermute x8, waiting for transfers between devices, with_halo(): lax.ppermute(tail, axis, [(i, (i + 1) % count) for i in range(count)])  59.3 us
    psum x1, blocking collectives, by_each_axis(): half = lax.psum(value, leading)  45.1 us
    dot_general x28, matrix products, local_apply(): jnp.einsum('xyrb,xyba->xyra', piece, blocks[:, :, slot], preferred_elemen...  23.2 us
    ppermute x8, starting transfers between devices, with_halo(): lax.ppermute(tail, axis, [(i, (i + 1) % count) for i in range(count)])  18.6 us
  transfers between devices with their start and end apart: 16, of which 11 were waited for; matrix products, arithmetic and copies ran while one was open for 2% of the time, Pallas kernels for 0%

profile of v1, /device:TPU:8, one launch (start us, length us, event | category | flops | bytes accessed | tf_op | source)
XLA Modules:
  0.0 459.4 jit_solution(13410557057187684822)
XLA Ops:
  1.5 3.5 collective-permute-start
  5.0 6.2 %collective-permute-start.1 = (bf16[1,2,128,128]{3,2,1,0:T(8,128)(2,1)S(1)}, bf16[1,2,128,128]{3,2,1,0:T(8,128)(2,1)S(1)}, u32[]{:S(2)}, u32[]{:S(2)}) collective-permute-start(bf16[1,2,128,128]{3,2,1,0:T(8,128)(2,1)S(1)} %get-tuple-element.53), channel_id=1, source_target_pairs={{16,0},{32,16},{48,32},{64,48},{80,64},{96,80},{112,96},{128,112},... | collective-permute-start | bytes 196616 | tf_op jit(solution)/shard_map/ppermute | solution.py:23
  19.0 8.2 %collective-permute-start.3 = (bf16[6,1,128,128]{3,2,1,0:T(8,128)(2,1)S(1)}, bf16[6,1,128,128]{3,2,1,0:T(8,128)(2,1)S(1)}, u32[]{:S(2)}, u32[]{:S(2)}) collective-permute-start(bf16[6,1,128,128]{3,2,1,0:T(8,128)(2,1)S(1)} %get-tuple-element.46), channel_id=1, source_target_pairs={{1,0},{2,1},{3,2},{4,3},{5,4},{6,5},{7,6},{8,7},{9,8},{10,9},{11,1... | collective-permute-start | bytes 589832 | tf_op jit(solution)/shard_map/ppermute | solution.py:23
  27.2 1.9 collective-permute-start.2
  30.4 10.4 %collective-permute-done.2 = bf16[6,1,128,128]{3,2,1,0:T(8,128)(2,1)S(1)} collective-permute-done((bf16[6,1,128,128]{3,2,1,0:T(8,128)(2,1)S(1)}, bf16[6,1,128,128]{3,2,1,0:T(8,128)(2,1)S(1)}, u32[]{:S(2)}, u32[]{:S(2)}) %collective-permute-start.2) | collective-permute-done | bytes 196640 | tf_op jit(solution)/shard_map/ppermute | solution.py:21
  52.7 15.3 %collective-permute-start.5 = (bf16[1,2,128,128]{2,3,1,0:T(8,128)(2,1)S(1)}, bf16[1,2,128,128]{2,3,1,0:T(8,128)(2,1)S(1)}, u32[]{:S(2)}, u32[]{:S(2)}) collective-permute-start(bf16[1,2,128,128]{2,3,1,0:T(8,128)(2,1)S(1)} %get-tuple-element.52), channel_id=1, source_target_pairs={{16,0},{32,16},{48,32},{64,48},{80,64},{96,80},{112,96},{128,112},... | collective-permute-start | bytes 196616 | tf_op jit(solution)/shard_map/ppermute | solution.py:23
  68.0 1.9 collective-permute-start.4
  70.0 10.8 %collective-permute-done.4 = bf16[1,2,128,128]{2,3,1,0:T(8,128)(2,1)S(1)} collective-permute-done((bf16[1,2,128,128]{2,3,1,0:T(8,128)(2,1)S(1)}, bf16[1,2,128,128]{2,3,1,0:T(8,128)(2,1)S(1)}, u32[]{:S(2)}, u32[]{:S(2)}) %collective-permute-start.4) | collective-permute-done | bytes 65568 | tf_op jit(solution)/shard_map/ppermute | solution.py:21
  81.5 1.9 collective-permute-start.7
  83.4 2.4 collective-permute-start.6
  88.0 9.0 %collective-permute-done.6 = bf16[6,1,128,128]{2,3,1,0:T(8,128)(2,1)} collective-permute-done((bf16[6,1,128,128]{2,3,1,0:T(8,128)(2,1)S(1)}, bf16[6,1,128,128]{2,3,1,0:T(8,128)(2,1)}, u32[]{:S(2)}, u32[]{:S(2)}) %collective-permute-start.6) | collective-permute-done | bytes 196640 | tf_op jit(solution)/shard_map/ppermute | solution.py:21
  99.0 1.4 gather_fusion.8
  100.4 1.4 gather_fusion.9
  101.8 1.4 gather_fusion.10
  103.3 1.4 gather_fusion.11
  104.7 1.4 gather_fusion.12
  109.6 1.8 copy.264
  111.4 1.8 copy.265
  113.3 1.8 copy.266
  115.1 1.8 copy.267
  124.1 17.1 %collective-permute-start.9 = (bf16[1,2,128,128]{2,3,1,0:T(8,128)(2,1)S(1)}, bf16[1,2,128,128]{2,3,1,0:T(8,128)(2,1)S(1)}, u32[]{:S(2)}, u32[]{:S(2)}) collective-permute-start(bf16[1,2,128,128]{2,3,1,0:T(8,128)(2,1)S(1)} %get-tuple-element.50), channel_id=1, source_target_pairs={{16,0},{32,16},{48,32},{64,48},{80,64},{96,80},{112,96},{128,112},... | collective-permute-start | bytes 196616 | tf_op jit(solution)/shard_map/ppermute | solution.py:23
  141.2 1.9 collective-permute-start.8
  143.1 4.2 collective-permute-done.8
  147.5 1.9 collective-permute-start.11
  149.4 2.4 collective-permute-start.10
  152.8 10.2 %collective-permute-done.10 = bf16[6,1,128,128]{2,3,1,0:T(8,128)(2,1)S(1)} collective-permute-done((bf16[6,1,128,128]{2,3,1,0:T(8,128)(2,1)S(1)}, bf16[6,1,128,128]{2,3,1,0:T(8,128)(2,1)S(1)}, u32[]{:S(2)}, u32[]{:S(2)}) %collective-permute-start.10) | collective-permute-done | bytes 196640 | tf_op jit(solution)/shard_map/ppermute | solution.py:21
  172.2 1.8 copy.270
  175.4 1.8 copy.271
  177.2 1.8 copy.272
  179.0 1.8 copy.273
  180.8 1.8 copy.274
  184.6 1.4 fusion.15
  186.0 1.4 fusion.14
  189.9 15.0 %collective-permute-start.13 = (bf16[1,2,128,128]{2,3,1,0:T(8,128)(2,1)S(1)}, bf16[1,2,128,128]{2,3,1,0:T(8,128)(2,1)S(1)}, u32[]{:S(2)}, u32[]{:S(2)}) collective-permute-start(bf16[1,2,128,128]{2,3,1,0:T(8,128)(2,1)S(1)} %get-tuple-element.48), channel_id=1, source_target_pairs={{16,0},{32,16},{48,32},{64,48},{80,64},{96,80},{112,96},{128,112},... | collective-permute-start | bytes 196616 | tf_op jit(solution)/shard_map/ppermute | solution.py:23
  204.9 1.9 collective-permute-start.12
  206.8 4.2 collective-permute-done.12
  211.1 1.9 collective-permute-start.15
  213.1 2.6 collective-permute-start.14
  216.3 10.5 %collective-permute-done.14 = bf16[6,1,128,128]{2,3,1,0:T(8,128)(2,1)S(1)} collective-permute-done((bf16[6,1,128,128]{2,3,1,0:T(8,128)(2,1)S(1)}, bf16[6,1,128,128]{2,3,1,0:T(8,128)(2,1)S(1)}, u32[]{:S(2)}, u32[]{:S(2)}) %collective-permute-start.14) | collective-permute-done | bytes 196640 | tf_op jit(solution)/shard_map/ppermute | solution.py:21
  236.0 1.8 copy.277
  239.1 1.8 copy.278
  241.8 1.8 copy.280
  243.6 1.8 copy.281
  245.4 1.8 copy.282
  248.3 1.4 fusion.7
  249.7 1.4 fusion.6
  253.2 45.1 %all-reduce.1 = (f32[128]{0:T(128)S(1)}, f32[128]{0:T(128)S(1)}, f32[128]{0:T(128)S(1)}, f32[128]{0:T(128)S(1)}, f32[128]{0:T(128)S(1)}) all-reduce(f32[128]{0:T(128)S(1)} %get-tuple-element.13, f32[128]{0:T(128)S(1)} %get-tuple-element.10, f32[128]{0:T(128)S(1)} %get-tuple-element.11, ...), channel_id=1, replica_groups=mesh['gx'=32,'gy'=16] {'gy'}, use_global_device_ids=true, to_apply=%region_1.2 | all-reduce | flops 640 | bytes 5120 | tf_op jit(solution)/shard_map/psum | solution.py:10
  298.3 159.6 %all-reduce = (f32[1,128]{1,0:T(1,128)S(1)}, f32[1,128]{1,0:T(1,128)S(1)}, f32[1,128]{1,0:T(1,128)S(1)}, f32[1,128]{1,0:T(1,128)S(1)}, f32[1,128]{1,0:T(1,128)S(1)}) all-reduce(f32[1,128]{1,0:T(1,128)S(1)} %bitcast.255, f32[1,128]{1,0:T(1,128)S(1)} %bitcast.256, f32[1,128]{1,0:T(1,128)S(1)} %bitcast.257, ...), channel_id=1, replica_groups=mesh['gx'=32,'gy'=16] {'gx'}, use_global_device_ids=true, to_apply=%region_2.3 | all-reduce | flops 640 | bytes 5120 | tf_op jit(solution)/shard_map/psum | solution.py:11
  (262 shorter events, 69.8 us)
Async XLA Ops:
  1.5 16.4 %collective-permute-start = (bf16[1,2,128,128]{3,2,1,0:T(8,128)(2,1)S(1)}, bf16[1,2,128,128]{3,2,1,0:T(8,128)(2,1)S(1)}, u32[]{:S(2)}, u32[]{:S(2)}) collective-permute-start(bf16[1,2,128,128]{3,2,1,0:T(8,128)(2,1)S(1)} %get-tuple-element.54), channel_id=1, source_target_pairs={{0,16},{16,32},{32,48},{48,64},{64,80},{80,96},{96,112},{112,128},... | collective-permute-start | bytes 196616 | tf_op jit(solution)/shard_map/ppermute | solution.py:21
  5.0 13.9 %collective-permute-start.1 = (bf16[1,2,128,128]{3,2,1,0:T(8,128)(2,1)S(1)}, bf16[1,2,128,128]{3,2,1,0:T(8,128)(2,1)S(1)}, u32[]{:S(2)}, u32[]{:S(2)}) collective-permute-start(bf16[1,2,128,128]{3,2,1,0:T(8,128)(2,1)S(1)} %get-tuple-element.53), channel_id=1, source_target_pairs={{16,0},{32,16},{48,32},{64,48},{80,64},{96,80},{112,96},{128,112},... | collective-permute-start | bytes 196616 | tf_op jit(solution)/shard_map/ppermute | solution.py:23
  15.2 32.7 %copy-start.52 = (pred[4,2]{1,0:T(4,128)(4,1)}, pred[4,2]{1,0:T(4,128)(4,1)S(1)}, u32[]{:S(2)}) copy-start(pred[4,2]{1,0:T(4,128)(4,1)S(1)} %get-tuple-element.79) | copy-start | bytes 28
  15.2 36.7 %copy-start.50 = (pred[4,2]{1,0:T(4,128)(4,1)}, pred[4,2]{1,0:T(4,128)(4,1)S(1)}, u32[]{:S(2)}) copy-start(pred[4,2]{1,0:T(4,128)(4,1)S(1)} %get-tuple-element.26) | copy-start | bytes 28
  16.8 32.5 %copy-start.48 = (pred[4,2]{1,0:T(4,128)(4,1)}, pred[4,2]{1,0:T(4,128)(4,1)S(1)}, u32[]{:S(2)}) copy-start(pred[4,2]{1,0:T(4,128)(4,1)S(1)} %get-tuple-element.69) | copy-start | bytes 28
  16.9 33.9 %copy-start.46 = (pred[4,2]{1,0:T(4,128)(4,1)}, pred[4,2]{1,0:T(4,128)(4,1)S(1)}, u32[]{:S(2)}) copy-start(pred[4,2]{1,0:T(4,128)(4,1)S(1)} %get-tuple-element.71) | copy-start | bytes 28
  16.9 34.2 %copy-start.44 = (pred[4,2]{1,0:T(4,128)(4,1)}, pred[4,2]{1,0:T(4,128)(4,1)S(1)}, u32[]{:S(2)}) copy-start(pred[4,2]{1,0:T(4,128)(4,1)S(1)} %get-tuple-element.73) | copy-start | bytes 28
  16.9 34.6 %copy-start.42 = (pred[4,2]{1,0:T(4,128)(4,1)}, pred[4,2]{1,0:T(4,128)(4,1)S(1)}, u32[]{:S(2)}) copy-start(pred[4,2]{1,0:T(4,128)(4,1)S(1)} %get-tuple-element.75) | copy-start | bytes 28
  16.9 35.4 %copy-start.54 = (pred[4,2]{1,0:T(4,128)(4,1)}, pred[4,2]{1,0:T(4,128)(4,1)S(1)}, u32[]{:S(2)}) copy-start(pred[4,2]{1,0:T(4,128)(4,1)S(1)} %get-tuple-element.24) | copy-start | bytes 28
  17.8 34.5 %copy-start.26 = (f32[4,2]{1,0:T(4,128)}, f32[4,2]{1,0:T(4,128)S(1)}, u32[]{:S(2)}) copy-start(f32[4,2]{1,0:T(4,128)S(1)} %copy.253) | copy-start | bytes 100
  17.8 24.4 %copy-start.30 = (s32[1024]{0:T(1024)}, s32[1024]{0:T(1024)S(1)}, u32[]{:S(2)}) copy-start(s32[1024]{0:T(1024)S(1)} %get-tuple-element.105) | copy-start | bytes 12292
  17.8 25.7 %copy-start.28 = (s32[1024]{0:T(1024)}, s32[1024]{0:T(1024)S(1)}, u32[]{:S(2)}) copy-start(s32[1024]{0:T(1024)S(1)} %get-tuple-element.104) | copy-start | bytes 12292
  17.8 27.0 %copy-start.34 = (s32[1024]{0:T(1024)}, s32[1024]{0:T(1024)S(1)}, u32[]{:S(2)}) copy-start(s32[1024]{0:T(1024)S(1)} %get-tuple-element.103) | copy-start | bytes 12292
  17.8 28.3 %copy-start.32 = (s32[1024]{0:T(1024)}, s32[1024]{0:T(1024)S(1)}, u32[]{:S(2)}) copy-start(s32[1024]{0:T(1024)S(1)} %get-tuple-element.102) | copy-start | bytes 12292
  17.8 28.8 %copy-start.38 = (s32[1024]{0:T(1024)}, s32[1024]{0:T(1024)S(1)}, u32[]{:S(2)}) copy-start(s32[1024]{0:T(1024)S(1)} %get-tuple-element.101) | copy-start | bytes 12292
  17.9 29.4 %copy-start.36 = (s32[1024]{0:T(1024)}, s32[1024]{0:T(1024)S(1)}, u32[]{:S(2)}) copy-start(s32[1024]{0:T(1024)S(1)} %get-tuple-element.100) | copy-start | bytes 12292
  17.9 24.3 %copy-start.40 = (s32[1024]{0:T(1024)}, s32[1024]{0:T(1024)S(1)}, u32[]{:S(2)}) copy-start(s32[1024]{0:T(1024)S(1)} %pad_clamp_fusion.6) | copy-start | bytes 12292
  19.0 11.4 %collective-permute-start.3 = (bf16[6,1,128,128]{3,2,1,0:T(8,128)(2,1)S(1)}, bf16[6,1,128,128]{3,2,1,0:T(8,128)(2,1)S(1)}, u32[]{:S(2)}, u32[]{:S(2)}) collective-permute-start(bf16[6,1,128,128]{3,2,1,0:T(8,128)(2,1)S(1)} %get-tuple-element.46), channel_id=1, source_target_pairs={{1,0},{2,1},{3,2},{4,3},{5,4},{6,5},{7,6},{8,7},{9,8},{10,9},{11,1... | collective-permute-start | bytes 589832 | tf_op jit(solution)/shard_map/ppermute | solution.py:23
  27.2 13.6 %collective-permute-start.2 = (bf16[6,1,128,128]{3,2,1,0:T(8,128)(2,1)S(1)}, bf16[6,1,128,128]{3,2,1,0:T(8,128)(2,1)S(1)}, u32[]{:S(2)}, u32[]{:S(2)}) collective-permute-start(bf16[6,1,128,128]{3,2,1,0:T(8,128)(2,1)S(1)} %get-tuple-element.45), channel_id=1, source_target_pairs={{0,1},{1,2},{2,3},{3,4},{4,5},{5,6},{6,7},{7,8},{8,9},{9,10},{10,1... | collective-permute-start | bytes 589832 | tf_op jit(solution)/shard_map/ppermute | solution.py:21
  29.2 18.8 %copy-start.24 = (f32[4,2]{1,0:T(4,128)}, f32[4,2]{1,0:T(4,128)S(1)}, u32[]{:S(2)}) copy-start(f32[4,2]{1,0:T(4,128)S(1)} %get-tuple-element.64) | copy-start | bytes 100
  29.2 22.0 %copy-start.22 = (f32[4,2]{1,0:T(4,128)}, f32[4,2]{1,0:T(4,128)S(1)}, u32[]{:S(2)}) copy-start(f32[4,2]{1,0:T(4,128)S(1)} %get-tuple-element.63) | copy-start | bytes 100
  40.9 7.0 %copy-start = (bf16[4,2,7,128,128]{4,3,2,1,0:T(8,128)(2,1)S(1)}, bf16[4,2,7,128,128]{4,3,2,1,0:T(8,128)(2,1)}, u32[]{:S(2)}) copy-start(bf16[4,2,7,128,128]{4,3,2,1,0:T(8,128)(2,1)} %param.7) | copy-start | bytes 5505028
  52.3 33.5 %copy-start.4 = (bf16[4,2,128,128]{3,2,1,0:T(8,128)(2,1)S(1)}, bf16[4,2,128,128]{3,2,1,0:T(8,128)(2,1)}, u32[]{:S(2)}) copy-start(bf16[4,2,128,128]{3,2,1,0:T(8,128)(2,1)} %param.6) | copy-start | bytes 786436
  52.7 17.2 %collective-permute-start.5 = (bf16[1,2,128,128]{2,3,1,0:T(8,128)(2,1)S(1)}, bf16[1,2,128,128]{2,3,1,0:T(8,128)(2,1)S(1)}, u32[]{:S(2)}, u32[]{:S(2)}) collective-permute-start(bf16[1,2,128,128]{2,3,1,0:T(8,128)(2,1)S(1)} %get-tuple-element.52), channel_id=1, source_target_pairs={{16,0},{32,16},{48,32},{64,48},{80,64},{96,80},{112,96},{128,112},... | collective-permute-start | bytes 196616 | tf_op jit(solution)/shard_map/ppermute | solution.py:23
  68.0 12.7 %collective-permute-start.4 = (bf16[1,2,128,128]{2,3,1,0:T(8,128)(2,1)S(1)}, bf16[1,2,128,128]{2,3,1,0:T(8,128)(2,1)S(1)}, u32[]{:S(2)}, u32[]{:S(2)}) collective-permute-start(bf16[1,2,128,128]{2,3,1,0:T(8,128)(2,1)S(1)} %get-tuple-element.51), channel_id=1, source_target_pairs={{0,16},{16,32},{32,48},{48,64},{64,80},{80,96},{96,112},{112,128},... | collective-permute-start | bytes 196616 | tf_op jit(solution)/shard_map/ppermute | solution.py:21
  81.5 5.9 %collective-permute-start.7 = (bf16[6,1,128,128]{2,3,1,0:T(8,128)(2,1)}, bf16[6,1,128,128]{2,3,1,0:T(8,128)(2,1)S(1)}, u32[]{:S(2)}, u32[]{:S(2)}) collective-permute-start(bf16[6,1,128,128]{2,3,1,0:T(8,128)(2,1)} %get-tuple-element.44), channel_id=1, source_target_pairs={{1,0},{2,1},{3,2},{4,3},{5,4},{6,5},{7,6},{8,7},{9,8},{10,9},{11,1... | collective-permute-start | bytes 589832 | tf_op jit(solution)/shard_map/ppermute | solution.py:23
  83.4 13.7 %collective-permute-start.6 = (bf16[6,1,128,128]{2,3,1,0:T(8,128)(2,1)S(1)}, bf16[6,1,128,128]{2,3,1,0:T(8,128)(2,1)}, u32[]{:S(2)}, u32[]{:S(2)}) collective-permute-start(bf16[6,1,128,128]{2,3,1,0:T(8,128)(2,1)S(1)} %get-tuple-element.43), channel_id=1, source_target_pairs={{0,1},{1,2},{2,3},{3,4},{4,5},{5,6},{6,7},{7,8},{8,9},{9,10},{10,1... | collective-permute-start | bytes 589832 | tf_op jit(solution)/shard_map/ppermute | solution.py:21
  98.2 7.9 %copy-start.37 = (s32[1024]{0:T(1024)S(1)}, s32[1024]{0:T(1024)}, u32[]{:S(2)}) copy-start(s32[1024]{0:T(1024)} %copy-done.36) | copy-start | bytes 12292
  99.0 9.3 %copy-start.25 = (f32[4,2]{1,0:T(4,128)S(1)}, f32[4,2]{1,0:T(4,128)}, u32[]{:S(2)}) copy-start(f32[4,2]{1,0:T(4,128)} %copy-done.24) | copy-start | bytes 100
  99.0 9.3 %copy-start.53 = (pred[4,2]{1,0:T(4,128)(4,1)S(1)}, pred[4,2]{1,0:T(4,128)(4,1)}, u32[]{:S(2)}) copy-start(pred[4,2]{1,0:T(4,128)(4,1)} %copy-done.52) | copy-start | bytes 28
  107.4 9.5 %copy-start.7 = (bf16[8,128,128]{1,2,0:T(8,128)(2,1)S(1)}, bf16[8,128,128]{1,2,0:T(8,128)(2,1)}, u32[]{:S(2)}) copy-start(bf16[8,128,128]{1,2,0:T(8,128)(2,1)} %gather_fusion.12) | copy-start | bytes 786436
  108.3 9.5 %copy-start.6 = (bf16[8,128,128]{1,2,0:T(8,128)(2,1)S(1)}, bf16[8,128,128]{1,2,0:T(8,128)(2,1)}, u32[]{:S(2)}) copy-start(bf16[8,128,128]{1,2,0:T(8,128)(2,1)} %gather_fusion.13) | copy-start | bytes 786436
  109.6 9.0 %copy-start.49 = (pred[4,2]{1,0:T(4,128)(4,1)S(1)}, pred[4,2]{1,0:T(4,128)(4,1)}, u32[]{:S(2)}) copy-start(pred[4,2]{1,0:T(4,128)(4,1)} %copy-done.48) | copy-start | bytes 28
  124.1 39.0 %copy-start.41 = (s32[1024]{0:T(1024)S(1)}, s32[1024]{0:T(1024)}, u32[]{:S(2)}) copy-start(s32[1024]{0:T(1024)} %copy-done.40) | copy-start | bytes 12292
  124.1 19.0 %collective-permute-start.9 = (bf16[1,2,128,128]{2,3,1,0:T(8,128)(2,1)S(1)}, bf16[1,2,128,128]{2,3,1,0:T(8,128)(2,1)S(1)}, u32[]{:S(2)}, u32[]{:S(2)}) collective-permute-start(bf16[1,2,128,128]{2,3,1,0:T(8,128)(2,1)S(1)} %get-tuple-element.50), channel_id=1, source_target_pairs={{16,0},{32,16},{48,32},{64,48},{80,64},{96,80},{112,96},{128,112},... | collective-permute-start | bytes 196616 | tf_op jit(solution)/shard_map/ppermute | solution.py:23
  141.2 23.2 %copy-start.31 = (s32[1024]{0:T(1024)S(1)}, s32[1024]{0:T(1024)}, u32[]{:S(2)}) copy-start(s32[1024]{0:T(1024)} %copy-done.30) | copy-start | bytes 12292
  141.2 6.2 %collective-permute-start.8 = (bf16[1,2,128,128]{2,3,1,0:T(8,128)(2,1)S(1)}, bf16[1,2,128,128]{2,3,1,0:T(8,128)(2,1)S(1)}, u32[]{:S(2)}, u32[]{:S(2)}) collective-permute-start(bf16[1,2,128,128]{2,3,1,0:T(8,128)(2,1)S(1)} %get-tuple-element.49), channel_id=1, source_target_pairs={{0,16},{16,32},{32,48},{48,64},{64,80},{80,96},{96,112},{112,128},... | collective-permute-start | bytes 196616 | tf_op jit(solution)/shard_map/ppermute | solution.py:21
  147.4 18.3 %copy-start.29 = (s32[1024]{0:T(1024)S(1)}, s32[1024]{0:T(1024)}, u32[]{:S(2)}) copy-start(s32[1024]{0:T(1024)} %copy-done.28) | copy-start | bytes 12292
  147.4 19.6 %copy-start.35 = (s32[1024]{0:T(1024)S(1)}, s32[1024]{0:T(1024)}, u32[]{:S(2)}) copy-start(s32[1024]{0:T(1024)} %copy-done.34) | copy-start | bytes 12292
  147.5 5.4 %collective-permute-start.11 = (bf16[6,1,128,128]{2,3,1,0:T(8,128)(2,1)S(1)}, bf16[6,1,128,128]{2,3,1,0:T(8,128)(2,1)S(1)}, u32[]{:S(2)}, u32[]{:S(2)}) collective-permute-start(bf16[6,1,128,128]{2,3,1,0:T(8,128)(2,1)S(1)} %get-tuple-element.42), channel_id=1, source_target_pairs={{1,0},{2,1},{3,2},{4,3},{5,4},{6,5},{7,6},{8,7},{9,8},{10,9},{11,1... | collective-permute-start | bytes 589832 | tf_op jit(solution)/shard_map/ppermute | solution.py:23
  149.4 18.9 %copy-start.33 = (s32[1024]{0:T(1024)S(1)}, s32[1024]{0:T(1024)}, u32[]{:S(2)}) copy-start(s32[1024]{0:T(1024)} %copy-done.32) | copy-start | bytes 12292
  149.4 20.2 %copy-start.39 = (s32[1024]{0:T(1024)S(1)}, s32[1024]{0:T(1024)}, u32[]{:S(2)}) copy-start(s32[1024]{0:T(1024)} %copy-done.38) | copy-start | bytes 12292
  149.4 13.6 %collective-permute-start.10 = (bf16[6,1,128,128]{2,3,1,0:T(8,128)(2,1)S(1)}, bf16[6,1,128,128]{2,3,1,0:T(8,128)(2,1)S(1)}, u32[]{:S(2)}, u32[]{:S(2)}) collective-permute-start(bf16[6,1,128,128]{2,3,1,0:T(8,128)(2,1)S(1)} %get-tuple-element.41), channel_id=1, source_target_pairs={{0,1},{1,2},{2,3},{3,4},{4,5},{5,6},{6,7},{7,8},{8,9},{9,10},{10,1... | collective-permute-start | bytes 589832 | tf_op jit(solution)/shard_map/ppermute | solution.py:21
  172.2 10.4 %copy-start.8 = (bf16[8,128,128]{1,2,0:T(8,128)(2,1)S(1)}, bf16[8,128,128]{1,2,0:T(8,128)(2,1)}, u32[]{:S(2)}) copy-start(bf16[8,128,128]{1,2,0:T(8,128)(2,1)} %gather_fusion.19) | copy-start | bytes 786436
  189.9 16.9 %collective-permute-start.13 = (bf16[1,2,128,128]{2,3,1,0:T(8,128)(2,1)S(1)}, bf16[1,2,128,128]{2,3,1,0:T(8,128)(2,1)S(1)}, u32[]{:S(2)}, u32[]{:S(2)}) collective-permute-start(bf16[1,2,128,128]{2,3,1,0:T(8,128)(2,1)S(1)} %get-tuple-element.48), channel_id=1, source_target_pairs={{16,0},{32,16},{48,32},{64,48},{80,64},{96,80},{112,96},{128,112},... | collective-permute-start | bytes 196616 | tf_op jit(solution)/shard_map/ppermute | solution.py:23
  204.9 6.2 %collective-permute-start.12 = (bf16[1,2,128,128]{2,3,1,0:T(8,128)(2,1)S(1)}, bf16[1,2,128,128]{2,3,1,0:T(8,128)(2,1)S(1)}, u32[]{:S(2)}, u32[]{:S(2)}) collective-permute-start(bf16[1,2,128,128]{2,3,1,0:T(8,128)(2,1)S(1)} %get-tuple-element.47), channel_id=1, source_target_pairs={{0,16},{16,32},{32,48},{48,64},{64,80},{80,96},{96,112},{112,128},... | collective-permute-start | bytes 196616 | tf_op jit(solution)/shard_map/ppermute | solution.py:21
  211.1 5.2 %collective-permute-start.15 = (bf16[6,1,128,128]{2,3,1,0:T(8,128)(2,1)S(1)}, bf16[6,1,128,128]{2,3,1,0:T(8,128)(2,1)S(1)}, u32[]{:S(2)}, u32[]{:S(2)}) collective-permute-start(bf16[6,1,128,128]{2,3,1,0:T(8,128)(2,1)S(1)} %get-tuple-element.40), channel_id=1, source_target_pairs={{1,0},{2,1},{3,2},{4,3},{5,4},{6,5},{7,6},{8,7},{9,8},{10,9},{11,1... | collective-permute-start | bytes 589832 | tf_op jit(solution)/shard_map/ppermute | solution.py:23
  213.1 13.8 %collective-permute-start.14 = (bf16[6,1,128,128]{2,3,1,0:T(8,128)(2,1)S(1)}, bf16[6,1,128,128]{2,3,1,0:T(8,128)(2,1)S(1)}, u32[]{:S(2)}, u32[]{:S(2)}) collective-permute-start(bf16[6,1,128,128]{2,3,1,0:T(8,128)(2,1)S(1)} %get-tuple-element.39), channel_id=1, source_target_pairs={{0,1},{1,2},{2,3},{3,4},{4,5},{5,6},{6,7},{7,8},{8,9},{9,10},{10,1... | collective-permute-start | bytes 589832 | tf_op jit(solution)/shard_map/ppermute | solution.py:21
  (24 other events, 50.8 us)
